TPU v7x, 32 devices: a whole 2x2x4 slice. The times are simulated.
32 devices in a mesh: parts: 2 (over y), tmpl: 4 (over z), sta: 2 (over x), sub: 2 (over core).
Axes of the slice: x: 2, y: 2, z: 4, core: 2. Of those that a mesh axis runs over, the one named last changes fastest.
Arguments:
- traces: bfloat16 [16, 3, 1536], P(('tmpl', 'sta'), None, ('parts', 'sub')), parts along dimension 2
- trace_tail: bfloat16 [16, 3, 726], P(('tmpl', 'sta'), None, 'parts'), parts along dimension 2
- templates: bfloat16 [32, 3, 300], P('tmpl')
- win_lengths: int32 [32], replicated, may hold values from 150 to 300
- moveouts: int32 [32, 16], replicated, may hold values from 0 to 63
- chan_mask: int32 [32, 3], P('parts'), parts along dimension 0, may hold values 0 or 1
- subnet: int32 [16], replicated, may hold values from 0 to 1
Outputs:
- network_stack: float32 [32, 2, 1536], P(('tmpl', 'sta'), None, ('parts', 'sub')), parts along dimension 2
There are 2 independent parts, one for each index of `parts`. A program takes and returns all parts, laid end to end along the dimension named above; an argument that names none is the same for every part. Nothing has to cross between parts.
All inputs are finite; a program needn't handle non-finite values.
Results may differ from a plain program's by a relative error of at most 0.0003.
Values may be sent and summed in bfloat16 or wider, within the bound.
A program may use at most 64 MiB of HBM per device.

v0:
```python
import jax
import jax.numpy as jnp
from jax import lax
from jax.sharding import PartitionSpec as P

REGIONS = 2


def shifted(block, axis, distance):
    devices = range(lax.axis_size(axis))
    route = [(i - distance, i) for i in devices if i - distance in devices]
    return lax.ppermute(block, axis, route)


def correlate(extended, tmpl_rows, win_rows, mask_rows, lag_rows, subnet_rows, t_out):
    span_len = tmpl_rows.shape[2]
    t_corr = extended.shape[2] - span_len + 1
    live_count = jnp.maximum(jnp.sum(mask_rows, axis=1), 1).astype(jnp.float32)
    weights = mask_rows.astype(jnp.float32)
    win_float = win_rows.astype(jnp.float32)
    running = jnp.zeros((extended.shape[0], tmpl_rows.shape[0], t_corr), jnp.float32)
    for channel in range(3):
        signal = extended[:, channel : channel + 1, :]
        corr = lax.conv_general_dilated(
            signal,
            tmpl_rows[:, channel : channel + 1, :],
            (1,),
            "VALID",
            dimension_numbers=("NCH", "OIH", "NCH"),
            preferred_element_type=jnp.float32,
        )
        squares = jnp.square(extended[:, channel, :].astype(jnp.float32))
        prefix = jnp.concatenate(
            [jnp.zeros((squares.shape[0], 1), jnp.float32), jnp.cumsum(squares, axis=1)], axis=1
        )

        def window_sum(width):
            return lax.dynamic_slice_in_dim(prefix, width, t_corr, 1) - prefix[:, :t_corr]

        energy = jax.vmap(window_sum, out_axes=1)(win_rows)
        tmpl_norm = jnp.sqrt(
            jnp.sum(jnp.square(tmpl_rows[:, channel, :].astype(jnp.float32)), axis=1) + 1e-06
        )
        denom = tmpl_norm[None, :, None] * jnp.sqrt(energy + 1e-05 * win_float[None, :, None])
        running = running + weights[:, channel][:, None, None] * corr / denom
    coherent = running / live_count[:, None, None]

    def align(series_rows, shift_rows):
        return jax.vmap(
            lambda series, lag_value: lax.dynamic_slice_in_dim(series, lag_value, t_out, 0)
        )(series_rows, shift_rows)

    aligned = jax.vmap(align)(coherent, jnp.transpose(lag_rows))
    member = (subnet_rows[:, None] == jnp.arange(REGIONS)[None, :]).astype(jnp.float32)
    return jnp.einsum("skt,sr->krt", aligned, member, precision=lax.Precision.HIGHEST)


def shards(traces, trace_tail, templates, win_lengths, moveouts, chan_mask, subnet):
    st_dev = traces.shape[0]
    t_dev = traces.shape[2]
    rim_len = trace_tail.shape[2]
    sub_index = lax.axis_index("sub")
    rim_cells = shifted(traces[:, :, :rim_len], "sub", -1)
    rim_cells = jnp.where(sub_index == lax.axis_size("sub") - 1, trace_tail, rim_cells)
    extended = jnp.concatenate([traces, rim_cells], axis=2)
    tmpl_count = lax.axis_size("tmpl")
    sta_count = lax.axis_size("sta")
    tmpl_index = lax.axis_index("tmpl")
    sta_index = lax.axis_index("sta")
    tmpl_dev = templates.shape[0]
    share_rows = tmpl_dev // sta_count
    own_lags = lax.dynamic_slice_in_dim(moveouts, tmpl_index * tmpl_dev, tmpl_dev, 0)
    own_lags = own_lags.reshape(tmpl_dev, tmpl_count, sta_count, st_dev)
    own_lags = lax.dynamic_index_in_dim(own_lags, sta_index, 2, False).reshape(
        tmpl_dev, tmpl_count * st_dev
    )
    group_mask = lax.dynamic_index_in_dim(
        chan_mask.reshape(tmpl_count, sta_count, st_dev, 3), sta_index, 1, False
    ).reshape(tmpl_count * st_dev, 3)
    group_subnet = lax.dynamic_index_in_dim(
        subnet.reshape(tmpl_count, sta_count, st_dev), sta_index, 1, False
    ).reshape(tmpl_count * st_dev)
    own_wins = lax.dynamic_slice_in_dim(win_lengths, tmpl_index * tmpl_dev, tmpl_dev, 0)
    zeros_init = jnp.zeros((tmpl_dev, REGIONS, t_dev), jnp.float32)
    stacked = zeros_init + correlate(
        lax.all_gather(extended, "tmpl", axis=0, tiled=True),
        templates,
        own_wins,
        group_mask,
        own_lags,
        group_subnet,
        t_dev,
    )
    summed = lax.psum(stacked, "sta")
    result = lax.dynamic_slice_in_dim(summed, sta_index * share_rows, share_rows, 0)
    return result


def solution(mesh):
    in_specs = (
        P(("tmpl", "sta"), None, ("parts", "sub")),
        P(("tmpl", "sta"), None, "parts"),
        P("tmpl", None, None),
        P(),
        P(),
        P("parts", None),
        P(),
    )
    out_specs = P(("tmpl", "sta"), None, ("parts", "sub"))
    return jax.shard_map(shards, mesh=mesh, in_specs=in_specs, out_specs=out_specs, check_vma=False)
```

profile of v0, /device:TPU:0, one launch (start us, length us, event | category | flops | bytes accessed | tf_op | source)
XLA Modules:
  0.0 337.7 jit_solution(7192902515686066570)
XLA Ops:
  11.4 14.8 %all_gather.3 = bf16[8,3,747]{2,1,0:T(4,128)(2,1)S(1)} all-gather(bf16[2,3,747]{2,1,0:T(4,128)(2,1)S(1)} %copy.152), channel_id=1, replica_groups=mesh['parts'=2,'tmpl'=4,'sta'=2,'sub'=2] {'tmpl'}, dimensions={0}, use_global_device_ids=true | all-gather | bytes 44820 | tf_op jit(solution)/shard_map/all_gather | solution.py:86
  32.2 11.5 %while.5 = (s32[]{:T(128)}, f32[8,748]{1,0:T(8,128)S(1)}, s32[8,2]{0,1:T(2,128)S(1)}, f32[8,8,448]{2,1,0:T(8,128)S(1)}, s32[]{:T(128)}) while((s32[]{:T(128)}, f32[8,748]{1,0:T(8,128)S(1)}, s32[8,2]{0,1:T(2,128)S(1)}, f32[8,8,448]{2,1,0:T(8,128)S(1)}, s32[]{:T(128)}) %tuple.70), condition=%wide.while_cond.1, body=%wide.while_body.1.sunk | while | flops 2 | bytes 32865 | solution.py:38
  46.7 9.8 %while.6 = (s32[]{:T(128)}, f32[8,748]{1,0:T(8,128)S(1)}, s32[8,2]{0,1:T(2,128)S(1)}, f32[8,8,448]{2,1,0:T(8,128)S(1)}, s32[]{:T(128)}) while((s32[]{:T(128)}, f32[8,748]{1,0:T(8,128)S(1)}, s32[8,2]{0,1:T(2,128)S(1)}, f32[8,8,448]{2,1,0:T(8,128)S(1)}, s32[]{:T(128)}) %tuple.79), condition=%wide.while_cond.2, body=%wide.while_body.2.sunk | while | flops 2 | bytes 32865 | solution.py:38
  60.1 15.6 %while.4 = (s32[]{:T(128)}, f32[8,748]{1,0:T(8,128)S(1)}, s32[8,2]{0,1:T(2,128)S(1)}, f32[8,8,448]{2,1,0:T(8,128)}, s32[]{:T(128)}) while((s32[]{:T(128)}, f32[8,748]{1,0:T(8,128)S(1)}, s32[8,2]{0,1:T(2,128)S(1)}, f32[8,8,448]{2,1,0:T(8,128)}, s32[]{:T(128)}) %tuple.80), condition=%wide.while_cond, body=%wide.while_body.sunk | while | flops 2 | bytes 31833 | solution.py:38
  75.7 26.1 %fusion.14 = f32[8,8,448]{1,0,2:T(8,128)S(1)} fusion(bf16[8,1,747]{0,1,2:T(2,128)(2,1)S(1)} %copy.154, bf16[8,1,300]{0,1,2:T(2,128)(2,1)S(1)} %copy.155), kind=kOutput, calls=%fused_computation.59 | convolution fusion | flops 17203200 | bytes 131440 | tf_op jit(solution)/shard_map/conv_general_dilated | solution.py:24
  102.5 25.8 %fusion.15 = f32[8,8,448]{1,0,2:T(8,128)S(1)} fusion(bf16[8,1,747]{0,1,2:T(2,128)(2,1)S(1)} %copy.161, bf16[8,1,300]{0,1,2:T(2,128)(2,1)S(1)} %copy.162), kind=kOutput, calls=%fused_computation.60 | convolution fusion | flops 17203200 | bytes 131440 | tf_op jit(solution)/shard_map/conv_general_dilated | solution.py:24
  129.0 25.9 %fusion.16 = f32[8,8,448]{1,0,2:T(8,128)S(1)} fusion(bf16[8,1,747]{0,1,2:T(2,128)(2,1)S(1)} %copy.168, bf16[8,1,300]{0,1,2:T(2,128)(2,1)S(1)} %copy.169), kind=kOutput, calls=%fused_computation.61 | convolution fusion | flops 17203200 | bytes 131440 | tf_op jit(solution)/shard_map/conv_general_dilated | solution.py:24
  157.1 171.2 %while.7 = (s32[]{:T(128)}, f32[8,8,448]{2,0,1:T(8,128)S(1)}, s32[64,3]{0,1:T(4,128)S(1)}, f32[64,384]{1,0:T(8,128)S(1)}, s32[]{:T(128)}, /*index=5*/s32[]{:T(128)}) while((s32[]{:T(128)}, f32[8,8,448]{2,0,1:T(8,128)S(1)}, s32[64,3]{0,1:T(4,128)S(1)}, f32[64,384]{1,0:T(8,128)S(1)}, s32[]{:T(128)}, /*index=5*/s32[]{:T(128)}) %tuple.82), condition=%wide.while_cond.3, body=%wide.while_body.3.sunk | while | flops 2 | bytes 6281 | solution.py:50
  157.8 2.0 dynamic-slice_bitcast_fusion.2
  160.5 2.0 dynamic-slice_bitcast_fusion.2
  163.2 2.0 dynamic-slice_bitcast_fusion.2
  165.8 2.0 dynamic-slice_bitcast_fusion.2
  168.5 2.0 dynamic-slice_bitcast_fusion.2
  171.2 2.0 dynamic-slice_bitcast_fusion.2
  173.9 2.0 dynamic-slice_bitcast_fusion.2
  176.5 2.0 dynamic-slice_bitcast_fusion.2
  179.2 2.0 dynamic-slice_bitcast_fusion.2
  181.9 2.0 dynamic-slice_bitcast_fusion.2
  184.6 2.0 dynamic-slice_bitcast_fusion.2
  187.2 2.0 dynamic-slice_bitcast_fusion.2
  189.9 2.0 dynamic-slice_bitcast_fusion.2
  192.6 2.0 dynamic-slice_bitcast_fusion.2
  195.3 2.0 dynamic-slice_bitcast_fusion.2
  198.0 2.0 dynamic-slice_bitcast_fusion.2
  200.6 2.0 dynamic-slice_bitcast_fusion.2
  203.3 2.0 dynamic-slice_bitcast_fusion.2
  206.0 2.0 dynamic-slice_bitcast_fusion.2
  208.7 2.0 dynamic-slice_bitcast_fusion.2
  211.3 2.0 dynamic-slice_bitcast_fusion.2
  214.0 2.0 dynamic-slice_bitcast_fusion.2
  216.7 2.0 dynamic-slice_bitcast_fusion.2
  219.4 2.0 dynamic-slice_bitcast_fusion.2
  222.0 2.0 dynamic-slice_bitcast_fusion.2
  224.7 2.0 dynamic-slice_bitcast_fusion.2
  227.4 2.0 dynamic-slice_bitcast_fusion.2
  230.1 2.0 dynamic-slice_bitcast_fusion.2
  232.7 2.0 dynamic-slice_bitcast_fusion.2
  235.4 2.0 dynamic-slice_bitcast_fusion.2
  238.1 2.0 dynamic-slice_bitcast_fusion.2
  240.8 2.0 dynamic-slice_bitcast_fusion.2
  243.4 2.0 dynamic-slice_bitcast_fusion.2
  246.1 2.0 dynamic-slice_bitcast_fusion.2
  248.8 2.0 dynamic-slice_bitcast_fusion.2
  251.5 2.0 dynamic-slice_bitcast_fusion.2
  254.1 2.0 dynamic-slice_bitcast_fusion.2
  256.8 2.0 dynamic-slice_bitcast_fusion.2
  259.5 2.0 dynamic-slice_bitcast_fusion.2
  262.2 2.0 dynamic-slice_bitcast_fusion.2
  264.8 2.0 dynamic-slice_bitcast_fusion.2
  267.5 2.0 dynamic-slice_bitcast_fusion.2
  270.2 2.0 dynamic-slice_bitcast_fusion.2
  272.9 2.0 dynamic-slice_bitcast_fusion.2
  275.5 2.0 dynamic-slice_bitcast_fusion.2
  278.2 2.0 dynamic-slice_bitcast_fusion.2
  280.9 2.0 dynamic-slice_bitcast_fusion.2
  283.6 2.0 dynamic-slice_bitcast_fusion.2
  286.3 2.0 dynamic-slice_bitcast_fusion.2
  291.6 2.0 dynamic-slice_bitcast_fusion.2
  297.0 2.0 dynamic-slice_bitcast_fusion.2
  302.3 2.0 dynamic-slice_bitcast_fusion.2
  307.7 2.0 dynamic-slice_bitcast_fusion.2
  313.0 2.0 dynamic-slice_bitcast_fusion.2
  318.4 2.0 dynamic-slice_bitcast_fusion.2
  328.6 8.3 %psum.7 = f32[8,2,384]{2,1,0:T(2,128)S(1)} all-reduce(f32[8,2,384]{2,1,0:T(2,128)S(1)} %convolution_bitcast_fusion), channel_id=1, replica_groups=mesh['parts'=2,'tmpl'=4,'sta'=2,'sub'=2] {'sta'}, use_global_device_ids=true, to_apply=%region_10.11 | all-reduce | flops 6144 | bytes 49152 | tf_op jit(solution)/shard_map/psum | solution.py:94
  (386 shorter events, 126.3 us)
Async XLA Ops:
  0.0 4.8 %copy-start = (s32[32,16]{0,1:T(8,128)S(1)}, s32[32,16]{0,1:T(8,128)}, u32[]{:S(2)}) copy-start(s32[32,16]{0,1:T(8,128)} %param.11) | copy-start | bytes 6148
  0.0 10.7 %collective-permute-start = (bf16[2,3,363]{2,0,1:T(2,128)(2,1)}, bf16[2,3,363]{2,0,1:T(2,128)(2,1)S(1)}, u32[]{:S(2)}, u32[]{:S(2)}) collective-permute-start(bf16[2,3,363]{2,0,1:T(2,128)(2,1)} %bitcast.121), channel_id=1, source_target_pairs={{1,0},{3,2},{5,4},{7,6},{9,8},{11,10},{13,12},{15,14},{17,16},{19,... | collective-permute-start | bytes 13076 | tf_op jit(solution)/shard_map/ppermute | solution.py:12
  43.7 16.5 %copy-start.1 = (f32[8,8,448]{2,1,0:T(8,128)}, f32[8,8,448]{2,1,0:T(8,128)S(1)}, u32[]{:S(2)}) copy-start(f32[8,8,448]{2,1,0:T(8,128)S(1)} %get-tuple-element.20) | copy-start | bytes 344068
  56.4 3.7 %copy-start.3 = (f32[8,8,448]{2,1,0:T(8,128)}, f32[8,8,448]{2,1,0:T(8,128)S(1)}, u32[]{:S(2)}) copy-start(f32[8,8,448]{2,1,0:T(8,128)S(1)} %get-tuple-element.28) | copy-start | bytes 344068
  154.9 0.9 copy-start.2
  154.9 1.0 copy-start.4
  154.9 1.0 copy-start.7
  154.9 1.0 copy-start.8
  154.9 1.0 copy-start.9
  154.9 0.9 copy-start.10
  154.9 0.9 copy-start.11
  154.9 0.9 copy-start.12
  155.0 0.9 copy-start.14
  155.0 0.9 copy-start.15
  155.0 0.9 copy-start.16
  155.0 0.9 copy-start.17
  155.0 0.9 copy-start.18
  155.0 2.1 copy-start.5
  155.0 2.1 copy-start.6
  155.0 173.4 %copy-start.13 = (s32[8]{0:T(128)S(1)}, s32[8]{0:T(128)}, u32[]{:S(2)}) copy-start(s32[8]{0:T(128)} %eq.18) | copy-start | bytes 100
where the time goes:
time: 343 us; the launch traced here: 338 us
  local copies, waits for them, and re-layouts  222 us (65%)
  matrix products  78 us (23%)
  blocking collectives  23.1 us (7%)
  other arithmetic  11.2 us (3%)
    gather x328, local copies, waits for them, and re-layouts  206 us
    conv_general_dilated x3, matrix products, correlate(): lax.conv_general_dilated(signal, tmpl_rows[:, channel:channel + 1, :], (1...  77.8 us
    all_gather x1, blocking collectives, shards(): lax.all_gather(extended, 'tmpl', axis=0, tiled=True)  14.8 us
    psum x1, blocking collectives, shards(): summed = lax.psum(stacked, 'sta')  8.29 us
  transfers between devices with their start and end apart: 1, of which 0 were waited for; matrix products, arithmetic and copies ran while one was open for 3% of the time, Pallas kernels for 0%

commit v1 on v0

v1 whole, which is shorter than its diff:
```python
import functools

import jax
import jax.numpy as jnp
from jax import lax
from jax.experimental import pallas as pl
from jax.experimental.pallas import tpu as pltpu
from jax.sharding import PartitionSpec as P

REGIONS = 2
CHANNELS = 3
LANES = 128
GROUP = 16
PITCH = 4
F32 = jnp.float32
BF16 = jnp.bfloat16
NT_DIMS = (((1,), (1,)), ((), ()))


def ceil_div(a, b):
    return -(-a // b)


def each(count, body):
    if count <= 16:
        for i in range(count):
            body(i)
    else:
        lax.fori_loop(0, count, lambda i, c: (body(i), c)[1], 0)


def kernel(
    n_sta, n_own, share,
    traces, tail, templates, wins, lags, mask, subnet,
    out,
    stage, send, recv, ebuf, tpad, wt, bt, acc, send_sem, recv_sem,
):
    st_dev, _, t_dev = traces.shape
    halo = tail.shape[2]
    span = templates.shape[2]
    lag_bits = (halo - span).bit_length()
    own_blocks = t_dev // LANES
    u_blocks = ceil_div(t_dev + halo - span + 1, LANES)
    k_blocks = ceil_div(LANES + span - 1, LANES)
    width = k_blocks * LANES
    owners = GROUP // st_dev
    n_groups = n_own // owners
    everyone = 2 * n_own

    t_me = lax.axis_index("tmpl")
    a_me = lax.axis_index("sta")
    u_me = lax.axis_index("sub")
    own = t_me * n_sta + a_me
    flat = own * 2 + u_me

    def place(d):
        other = lax.rem(flat + d, everyone)
        return {"tmpl": other // (2 * n_sta), "sta": (other // 2) % n_sta, "sub": other % 2}

    barrier = pltpu.get_barrier_semaphore()

    def greet(i):
        pl.semaphore_signal(barrier, inc=1, device_id=place(i + 1), device_id_type=pl.DeviceIdType.MESH)

    each(everyone - 1, greet)

    stage[...] = jnp.zeros_like(stage)
    for s in range(st_dev):
        rows = pl.ds(s * PITCH, CHANNELS)
        stage[0, rows, :] = traces[s].astype(F32)
        stage[1, rows, pl.ds(0, halo)] = tail[s].astype(F32)
    main = stage[0]
    rim = jnp.where(u_me == 1, main, stage[1])
    send[0] = main.astype(BF16)
    send[1] = rim.astype(BF16)
    recv[own, 0] = main.astype(BF16)

    pl.semaphore_wait(barrier, everyone - 1)

    def outgoing(i):
        d = i + 1
        half = d % 2
        return pltpu.make_async_remote_copy(
            src_ref=send.at[half],
            dst_ref=recv.at[own, half],
            send_sem=send_sem.at[i],
            recv_sem=recv_sem.at[i],
            device_id=place(d),
            device_id_type=pl.DeviceIdType.MESH,
        )

    each(everyone - 1, lambda i: outgoing(i).start())

    tpad[...] = jnp.zeros_like(tpad)
    for k in range(share):
        tpad[k, pl.ds(0, CHANNELS), pl.ds(0, span)] = templates[a_me * share + k].astype(F32)
    row_at = lax.broadcasted_iota(jnp.int32, (LANES, width), 0)
    col_at = lax.broadcasted_iota(jnp.int32, (LANES, width), 1)
    apart = col_at - row_at
    first = own * share
    inv_norm = []
    floor_rows = []
    for k in range(share):
        taps = tpad[k]
        power = jnp.sum(taps * taps, axis=1, keepdims=True)
        inv_norm.append(1.0 / jnp.sqrt(power + 1e-06))
        win = wins[first + k]
        floor_rows.append(jnp.full((1, LANES), 1e-05 * win.astype(F32), F32))
        band = jnp.logical_and(apart >= 0, apart < win)
        bt[pl.ds(k * LANES, LANES), :] = jnp.where(band, 1.0, 0.0).astype(BF16)
        for c in range(CHANNELS):
            line = jnp.broadcast_to(taps[c : c + 1, :], (LANES, width))
            slid = pltpu.roll(line, 0, 1, stride=1, stride_axis=0)
            wt[c, pl.ds(k * LANES, LANES), :] = slid.astype(BF16)
    floor_row = jnp.concatenate(floor_rows, axis=1)
    norm_rows = [
        jnp.concatenate(
            [jnp.broadcast_to(inv_norm[k][c : c + 1, :], (1, LANES)) for k in range(share)], axis=1
        )
        for c in range(CHANNELS)
    ]

    station_at = lax.broadcasted_iota(jnp.int32, (GROUP, LANES), 0)
    lane_at = lax.broadcasted_iota(jnp.int32, (share * GROUP, LANES), 1)

    def column(value_at):
        col = jnp.zeros((GROUP, LANES), jnp.int32)
        for s in range(GROUP):
            col = jnp.where(station_at == s, value_at(s), col)
        return col

    def prepare(group):
        base = group * GROUP
        lag = jnp.concatenate(
            [column(lambda s, k=k: lags[first + k, base + s]) for k in range(share)], axis=0
        )
        region = column(lambda s: subnet[base + s])
        open_ = mask[pl.ds(base, GROUP), :].astype(F32)
        live = jnp.maximum(jnp.sum(open_, axis=1, keepdims=True), 1.0)
        return lag, region, open_ / live

    def work(group, ready):
        lag, region, weight = ready
        for o in range(owners):
            for half in range(2):
                block = recv[group * owners + o, half].astype(F32)
                for n in range(own_blocks):
                    ebuf[half * own_blocks + n, pl.ds(o * st_dev * PITCH, st_dev * PITCH), :] = block[
                        :, n * LANES : (n + 1) * LANES
                    ]

        def spread(parts):
            empty = jnp.zeros_like(parts[0])
            parts = parts + [empty] * (u_blocks + k_blocks - 1 - len(parts))
            return jnp.concatenate(
                [jnp.concatenate(parts[j : j + u_blocks], axis=0) for j in range(k_blocks)], axis=1
            )

        corr = []
        squares = []
        for c in range(CHANNELS):
            wave = [ebuf[n, pl.ds(c, GROUP, stride=PITCH), :] for n in range(2 * own_blocks)]
            corr.append(
                lax.dot_general(
                    spread([w.astype(BF16) for w in wave]), wt[c], NT_DIMS, preferred_element_type=F32
                )
            )
            high = [(w * w).astype(BF16) for w in wave]
            low = [(w * w - h.astype(F32)).astype(BF16) for w, h in zip(wave, high)]
            squares.append(spread(high))
            squares.append(spread(low))
        energy = lax.dot_general(
            jnp.concatenate(squares, axis=0), bt[...], NT_DIMS, preferred_element_type=F32
        )
        tall = u_blocks * GROUP
        coherent = None
        for c in range(CHANNELS):
            at = 2 * c * tall
            power = energy[at : at + tall] + energy[at + tall : at + 2 * tall]
            scale = jnp.concatenate([weight[:, c : c + 1]] * u_blocks, axis=0)
            term = corr[c] * lax.rsqrt(power + floor_row) * (scale * norm_rows[c])
            coherent = term if coherent is None else coherent + term

        pieces = [
            jnp.concatenate(
                [
                    coherent[b * GROUP : (b + 1) * GROUP, k * LANES : (k + 1) * LANES]
                    for k in range(share)
                ],
                axis=0,
            )
            for b in range(u_blocks)
        ]
        for bit in range(lag_bits):
            step = 1 << bit
            turned = [pltpu.roll(p, LANES - step, 1) for p in pieces]
            stays = lane_at < LANES - step
            taken = (lax.shift_right_logical(lag, bit) & 1) == 1
            pieces = [
                jnp.where(
                    taken, jnp.where(stays, turned[b], turned[min(b + 1, u_blocks - 1)]), pieces[b]
                )
                for b in range(u_blocks)
            ]
        for k in range(share):
            for r in range(REGIONS):
                member = region == r
                total = jnp.concatenate(
                    [
                        jnp.sum(
                            jnp.where(member, pieces[n][k * GROUP : (k + 1) * GROUP], 0.0),
                            axis=0,
                            keepdims=True,
                        )
                        for n in range(own_blocks)
                    ],
                    axis=1,
                )
                if n_groups == 1:
                    out[k, pl.ds(r, 1), :] = total
                else:
                    acc[k, pl.ds(r, 1), :] += total

    if n_groups == 1:
        ready = prepare(0)
        each(everyone - 1, lambda i: outgoing(i).wait_recv())
        work(0, ready)
    else:
        acc[...] = jnp.zeros_like(acc)
        each(everyone - 1, lambda i: outgoing(i).wait_recv())

        def one(group, carry):
            work(group, prepare(group))
            return carry

        lax.fori_loop(0, n_groups, one, 0)
        out[...] = acc[...]
    each(everyone - 1, lambda i: outgoing(i).wait_send())


def shards(traces, trace_tail, templates, win_lengths, moveouts, chan_mask, subnet):
    n_tmpl = lax.axis_size("tmpl")
    n_sta = lax.axis_size("sta")
    n_own = n_tmpl * n_sta
    st_dev, _, t_dev = traces.shape
    halo = trace_tail.shape[2]
    span = templates.shape[2]
    share = templates.shape[0] // n_sta
    width = ceil_div(LANES + span - 1, LANES) * LANES
    block = (st_dev * PITCH, t_dev)
    vmem = pl.BlockSpec(memory_space=pltpu.VMEM)
    smem = pl.BlockSpec(memory_space=pltpu.SMEM)
    return pl.pallas_call(
        functools.partial(kernel, n_sta, n_own, share),
        out_shape=jax.ShapeDtypeStruct((share, REGIONS, t_dev), F32),
        in_specs=[vmem, vmem, vmem, smem, smem, vmem, smem],
        out_specs=vmem,
        scratch_shapes=[
            pltpu.VMEM((2,) + block, F32),
            pltpu.VMEM((2,) + block, BF16),
            pltpu.VMEM((n_own, 2) + block, BF16),
            pltpu.VMEM((2 * t_dev // LANES, GROUP * PITCH, LANES), F32),
            pltpu.VMEM((share, 8, width), F32),
            pltpu.VMEM((CHANNELS, share * LANES, width), BF16),
            pltpu.VMEM((share * LANES, width), BF16),
            pltpu.VMEM((share, REGIONS, t_dev), F32),
            pltpu.SemaphoreType.DMA((2 * n_own - 1,)),
            pltpu.SemaphoreType.DMA((2 * n_own - 1,)),
        ],
        compiler_params=pltpu.CompilerParams(
            collective_id=0, has_side_effects=True, vmem_limit_bytes=32 * 1024 * 1024
        ),
        name="matched_filter",
    )(traces, trace_tail, templates, win_lengths, moveouts, chan_mask, subnet)


def solution(mesh):
    in_specs = (
        P(("tmpl", "sta"), None, ("parts", "sub")),
        P(("tmpl", "sta"), None, "parts"),
        P("tmpl", None, None),
        P(),
        P(),
        P("parts", None),
        P(),
    )
    out_specs = P(("tmpl", "sta"), None, ("parts", "sub"))
    return jax.shard_map(shards, mesh=mesh, in_specs=in_specs, out_specs=out_specs, check_vma=False)
```

time: 343 us -> 15.1 us (0.04); the launches traced: 338 us -> 14.8 us
  local copies, waits for them, and re-layouts: 222 us -> 3.37 us
  matrix products: 78 us -> 0 us
  blocking collectives: 23.1 us -> 0 us
  Pallas kernels: 0 us -> 11.4 us
  other arithmetic: 11.2 us -> 0 us
    gather x329 -> x0, local copies, waits for them, and re-layouts: 207 us -> none
    conv_general_dilated x3 -> x0, matrix products: 77.8 us -> none  [correlate(): lax.conv_general_dilated(signal, tmpl_rows[:, channel:channel + 1, :], (1...]
    all_gather x1 -> x0, blocking collectives: 14.8 us -> none  [shards(): lax.all_gather(extended, 'tmpl', axis=0, tiled=True)]
    pallas_call x0 -> x1, Pallas kernels: none -> 11.4 us  [shards(): pl.pallas_call(functools.partial(kernel, n_sta, n_own, share), out_shape=...]
    psum x1 -> x0, blocking collectives: 8.29 us -> none  [shards(): summed = lax.psum(stacked, 'sta')]
    slice x14 -> x0, local copies, waits for them, and re-layouts: 7.09 us -> none  [the longest x4 2.86 us: correlate(): signal = extended[:, channel:channel + 1, :]]
    another operation x9 -> x0, other arithmetic: 5.84 us -> none
  transfers between devices with their start and end apart: 1 -> 0, of which waited for: 0 -> 0; matrix products, arithmetic and copies ran while one was open for 3% -> 0% of each run, Pallas kernels for 0% -> 0%
where the time goes in v1:
time: 15.1 us; the launch traced here: 14.8 us
  Pallas kernels  11.4 us (75%)
  local copies, waits for them, and re-layouts  3.37 us (22%)
    pallas_call x1, Pallas kernels, shards(): pl.pallas_call(functools.partial(kernel, n_sta, n_own, share), out_shape=...  11.4 us
    unnamed x18, local copies, waits for them, and re-layouts  3.37 us

profile of v1, /device:TPU:0, one launch (start us, length us, event | category | flops | bytes accessed | tf_op | source)
XLA Modules:
  0.0 14.8 jit_solution(17141516643328352328)
XLA Ops:
  0.0 0.0 copy-start.4
  0.0 0.7 %copy.8.traces = bf16[2,3,384]{2,1,0:T(4,128)(2,1)S(1)} copy(bf16[2,3,384]{2,0,1:T(2,128)(2,1)} %param.7) | data formatting | bytes 9216 | tf_op args[0]
  0.7 0.0 copy-done.4
  0.7 0.0 copy-start.5
  0.7 0.0 copy-start.3
  0.7 0.7 %copy-done.5 = s32[16,3]{0,1:T(4,128)S(1)} copy-done((s32[16,3]{0,1:T(4,128)S(1)}, s32[16,3]{0,1:T(4,128)}, u32[]{:S(2)}) %copy-start.5) | copy-done | bytes 216
  1.4 0.0 copy-start.2
  1.4 0.1 copy.12.mask
  1.5 0.0 copy-done.3
  1.5 0.1 copy.11.lags
  1.6 0.6 %copy-done.2 = bf16[8,3,300]{2,0,1:T(8,128)(2,1)S(1)} copy-done((bf16[8,3,300]{2,0,1:T(8,128)(2,1)S(1)}, bf16[8,3,300]{2,0,1:T(8,128)(2,1)}, u32[]{:S(2)}) %copy-start.2) | copy-done | bytes 14424
  2.1 0.0 copy-start
  2.1 0.0 copy-start.1
  2.1 0.6 %copy-done = s32[32]{0:T(128)S(1)} copy-done((s32[32]{0:T(128)S(1)}, s32[32]{0:T(128)}, u32[]{:S(2)}) %copy-start) | copy-done | bytes 152
  2.8 0.0 copy-done.1
  2.8 11.4 %matched_filter.1 = f32[4,2,384]{2,1,0:T(2,128)S(1)} custom-call(bf16[2,3,384]{2,1,0:T(4,128)(2,1)S(1)} %copy.8.traces, bf16[2,3,363]{2,1,0:T(4,128)(2,1)S(1)} %copy.9.tail, bf16[8,3,300]{2,1,0:T(4,128)(2,1)S(1)} %copy.10.templates, s32[32]{0:T(128)S(1)} %copy-done, s32[32,16]{1,0:T(8,128)S(1)} %copy.11.lags, s32[16,3]{1,0:T(8,128)S(1)} %copy.12.mask, ...), custom_call_target="tpu_custom_call" | custom-call | tf_op jit(solution)/shard_map/matched_filter/pallas_call | solution.py:253
  14.2 0.6 %copy.14 = f32[4,2,384]{2,1,0:T(2,128)} copy(f32[4,2,384]{2,1,0:T(2,128)S(1)} %matched_filter.1) | data formatting | bytes 24576
  (2 shorter events, 0.0 us)
Async XLA Ops:
  0.0 0.7 %copy-start.4 = (bf16[2,3,363]{2,0,1:T(2,128)(2,1)S(1)}, bf16[2,3,363]{2,0,1:T(2,128)(2,1)}, u32[]{:S(2)}) copy-start(bf16[2,3,363]{2,0,1:T(2,128)(2,1)} %param.8) | copy-start | bytes 13072
  0.7 0.7 %copy-start.5 = (s32[16,3]{0,1:T(4,128)S(1)}, s32[16,3]{0,1:T(4,128)}, u32[]{:S(2)}) copy-start(s32[16,3]{0,1:T(4,128)} %param.12) | copy-start | bytes 580
  0.7 0.8 %copy-start.3 = (s32[32,16]{0,1:T(8,128)S(1)}, s32[32,16]{0,1:T(8,128)}, u32[]{:S(2)}) copy-start(s32[32,16]{0,1:T(8,128)} %param.11) | copy-start | bytes 6148
  1.4 0.7 %copy-start.2 = (bf16[8,3,300]{2,0,1:T(8,128)(2,1)S(1)}, bf16[8,3,300]{2,0,1:T(8,128)(2,1)}, u32[]{:S(2)}) copy-start(bf16[8,3,300]{2,0,1:T(8,128)(2,1)} %param.9) | copy-start | bytes 43204
  2.1 0.7 %copy-start = (s32[32]{0:T(128)S(1)}, s32[32]{0:T(128)}, u32[]{:S(2)}) copy-start(s32[32]{0:T(128)} %wins.1) | copy-start | bytes 388
  2.1 0.7 %copy-start.1 = (s32[16]{0:T(128)S(1)}, s32[16]{0:T(128)}, u32[]{:S(2)}) copy-start(s32[16]{0:T(128)} %subnet.1) | copy-start | bytes 196
